TPU v7x, 512 devices: a whole 4x8x8 slice. The times are simulated.
512 devices in a mesh: dp: 2 (over core), ctx: 8 (over z_hi, x), exp: 32 (over z_lo, y).
Axes of the slice: x: 4, y: 8, z: 8 (z_hi: 2, z_lo: 4; z = z_hi * 4 + z_lo), core: 2. Of those that a mesh axis runs over, the one named last changes fastest.
Arguments:
- tokens: bfloat16 [65536, 2048], P(('dp', 'ctx', 'exp')), may hold values from -6 to 6
- cotangent: bfloat16 [65536, 2048], P(('dp', 'ctx', 'exp')), may hold values from -6 to 6
- expert_weights: bfloat16 [32, 768, 6144], P('exp', ('dp', 'ctx')), may hold values from -0.125 to 0.125
- route_ids: int32 [65536, 2], P(('dp', 'ctx', 'exp')), may hold values from 0 to 31, all different within a row; in each aligned block of 128 rows (0 to 127, 128 to 255, ...) at most 12 rows name the same one
- combine: float32 [65536, 2], P(('dp', 'ctx', 'exp')), may hold values from 0.1 to 1
Outputs:
- grad_tokens: bfloat16 [65536, 2048], P(('dp', 'ctx', 'exp'))
- grad_combine: float32 [65536, 2], P(('dp', 'ctx', 'exp'))
Inputs may be any that keep to these rules, and one draw needn't show every extreme that they name: `route_ids`: each token names 2 different experts; among the rows of one device no expert is named more than 12 times, a bound that some block reaches.
All inputs are finite; a program needn't handle non-finite values.
Results may differ from a plain program's by a relative error of at most 0.017.
Values may be sent and summed in bfloat16 or wider, within the bound.
A program may use at most 64 MiB of HBM per device.

v0:
```python
import jax
import jax.numpy as jnp
from jax import lax
from jax.sharding import PartitionSpec as P


def silu_parts(gate_pre):
    sigmoid_val = jax.nn.sigmoid(gate_pre)
    return (gate_pre * sigmoid_val, sigmoid_val * (1.0 + gate_pre * (1.0 - sigmoid_val)))


def hidden_terms(weight_piece, inputs):
    x_rows, dy_rows, row_scale = inputs
    model_width = x_rows.shape[1]
    unit_rows = weight_piece.reshape(-1, 3 * model_width)
    w_gate = unit_rows[:, :model_width]
    w_up = unit_rows[:, model_width : 2 * model_width]
    w_down = unit_rows[:, 2 * model_width :]
    contract = (((1,), (1,)), ((), ()))
    gate_pre = lax.dot_general(x_rows, w_gate, contract, preferred_element_type=jnp.float32)
    up_pre = lax.dot_general(x_rows, w_up, contract, preferred_element_type=jnp.float32)
    back_proj = lax.dot_general(dy_rows, w_down, contract, preferred_element_type=jnp.float32)
    active, slopes = silu_parts(gate_pre)
    comb_acc = jnp.sum(back_proj * active * up_pre, axis=1)
    d_hidden = row_scale[:, None] * back_proj
    d_gate = (d_hidden * up_pre * slopes).astype(jnp.bfloat16)
    d_up = (d_hidden * active).astype(jnp.bfloat16)
    grad_acc = jnp.dot(d_gate, w_gate, preferred_element_type=jnp.float32)
    grad_acc = grad_acc + jnp.dot(d_up, w_up, preferred_element_type=jnp.float32)
    return (grad_acc, comb_acc)


def body(tokens, cotangent, expert_weights, route_ids, combine):
    tok_rows, model_width = tokens.shape
    per_token = route_ids.shape[1]
    experts = lax.axis_size("exp")
    capacity = max(2, 3 * tok_rows * per_token // (2 * experts))
    slot_count = experts * capacity
    flat_ids = route_ids.reshape(-1)
    onehot = (flat_ids[:, None] == jnp.arange(experts, dtype=jnp.int32)[None, :]).astype(jnp.int32)
    ordinal = jnp.sum((jnp.cumsum(onehot, axis=0) - 1) * onehot, axis=1)
    target = flat_ids * capacity + ordinal
    placed = (target[:, None] == jnp.arange(slot_count, dtype=jnp.int32)[None, :]).astype(
        jnp.float32
    )
    by_token = jnp.sum(placed.reshape(tok_rows, per_token, slot_count), axis=1).astype(jnp.bfloat16)
    contract_rows = (((0,), (0,)), ((), ()))
    x_slots = lax.dot_general(
        by_token, tokens, contract_rows, preferred_element_type=jnp.float32
    ).astype(jnp.bfloat16)
    dy_slots = lax.dot_general(
        by_token, cotangent, contract_rows, preferred_element_type=jnp.float32
    ).astype(jnp.bfloat16)
    w_slots = jnp.sum(placed * combine.reshape(-1)[:, None], axis=0)
    x_recv, dy_recv, w_recv = (
        lax.all_to_all(
            x_slots.reshape(experts, capacity, model_width),
            "exp",
            split_axis=0,
            concat_axis=0,
            tiled=True,
        ),
        lax.all_to_all(
            dy_slots.reshape(experts, capacity, model_width),
            "exp",
            split_axis=0,
            concat_axis=0,
            tiled=True,
        ),
        lax.all_to_all(
            w_slots.reshape(experts, capacity).astype(jnp.bfloat16),
            "exp",
            split_axis=0,
            concat_axis=0,
            tiled=True,
        ).astype(jnp.float32),
    )
    inputs = (
        x_recv.reshape(slot_count, model_width),
        dy_recv.reshape(slot_count, model_width),
        w_recv.reshape(slot_count),
    )
    grad_slots, comb_slots = hidden_terms(
        lax.all_gather(expert_weights, ("dp", "ctx"), axis=1, tiled=True), inputs
    )
    grad_back, comb_back = (
        lax.all_to_all(
            grad_slots.astype(jnp.bfloat16).reshape(experts, capacity, model_width),
            "exp",
            split_axis=0,
            concat_axis=0,
            tiled=True,
        ),
        lax.all_to_all(
            comb_slots.reshape(experts, capacity).astype(jnp.bfloat16),
            "exp",
            split_axis=0,
            concat_axis=0,
            tiled=True,
        ).astype(jnp.float32),
    )
    grad_tokens = jnp.dot(
        by_token, grad_back.reshape(slot_count, model_width), preferred_element_type=jnp.float32
    ).astype(jnp.bfloat16)
    grad_combine = jnp.sum(placed * comb_back.reshape(-1)[None, :], axis=1).reshape(
        tok_rows, per_token
    )
    return (grad_tokens, grad_combine)


def solution(mesh):
    return jax.shard_map(
        body,
        mesh=mesh,
        in_specs=(
            P(("dp", "ctx", "exp"), None),
            P(("dp", "ctx", "exp"), None),
            P("exp", ("dp", "ctx"), None),
            P(("dp", "ctx", "exp"), None),
            P(("dp", "ctx", "exp"), None),
        ),
        out_specs=(P(("dp", "ctx", "exp"), None), P(("dp", "ctx", "exp"), None)),
        check_vma=False,
    )
```

profile of v0, /device:TPU:2, one launch (start us, length us, event | category | flops | bytes accessed | tf_op | source)
XLA Modules:
  0.0 340.6 jit_solution(13931619375600677401)
XLA Ops:
  7.2 0.0 copy-start
  7.2 0.0 all-gather.2.cloned.1.call-start
  7.2 0.7 all-gather.2.cloned.1.call-update
  7.9 0.8 copy.34
  8.7 0.1 eq.45
  8.8 0.1 eq.49
  9.0 0.6 reduce-window.6
  9.6 0.2 slice_reduce_fusion
  9.8 0.1 fusion.15
  9.9 0.1 reduce_sum.48
  10.1 0.1 copy.37
  10.1 0.7 multiply_add_fusion.1
  10.8 0.1 convert_reduce_fusion
  11.0 0.6 convolution_convert_fusion
  11.6 1.6 reshape.113
  13.2 13.0 %all-to-all-start.2 = ((bf16[32,12,2048]{2,1,0:T(8,128)(2,1)}), bf16[32,12,2048]{2,1,0:T(8,128)(2,1)S(1)}, u32[]{:S(2)}, u32[]{:S(2)}) async-start(bf16[32,12,2048]{2,1,0:T(8,128)(2,1)} %reshape.113), calls=%async_computation.2 | async-start | bytes 4194304 | tf_op jit(solution)/shard_map/all_to_all | solution.py:56
  26.2 1.7 convolution_convert_fusion.1
  28.0 3.6 %reshape.110 = bf16[32,12,2048]{2,1,0:T(8,128)(2,1)} reshape(bf16[384,2048]{1,0:T(8,128)(2,1)} %convolution_convert_fusion.1) | data formatting | bytes 3145728 | tf_op jit(solution)/shard_map/reshape | solution.py:64
  31.6 56.7 %all-to-all-done.2 = bf16[32,12,2048]{2,1,0:T(8,128)(2,1)S(1)} async-done(((bf16[32,12,2048]{2,1,0:T(8,128)(2,1)}), bf16[32,12,2048]{2,1,0:T(8,128)(2,1)S(1)}, u32[]{:S(2)}, u32[]{:S(2)}) %all-to-all-start.2) | async-done | bytes 1572896 | tf_op jit(solution)/shard_map/all_to_all | solution.py:56
  88.2 9.4 %all-to-all-start.1 = ((bf16[32,12,2048]{2,1,0:T(8,128)(2,1)}), bf16[32,12,2048]{2,1,0:T(8,128)(2,1)}, u32[]{:S(2)}, u32[]{:S(2)}) async-start(bf16[32,12,2048]{2,1,0:T(8,128)(2,1)} %reshape.110), calls=%async_computation.1 | async-start | bytes 4194304 | tf_op jit(solution)/shard_map/all_to_all | solution.py:63
  97.6 1.3 reshape.114
  98.9 97.1 %all-to-all-done.1 = bf16[32,12,2048]{2,1,0:T(8,128)(2,1)} async-done(((bf16[32,12,2048]{2,1,0:T(8,128)(2,1)}), bf16[32,12,2048]{2,1,0:T(8,128)(2,1)}, u32[]{:S(2)}, u32[]{:S(2)}) %all-to-all-start.1) | async-done | bytes 1572896 | tf_op jit(solution)/shard_map/all_to_all | solution.py:63
  196.0 3.7 %reshape.111 = bf16[384,2048]{1,0:T(8,128)(2,1)} reshape(bf16[32,12,2048]{2,1,0:T(8,128)(2,1)} %all-to-all-done.1) | data formatting | bytes 3145728 | tf_op jit(solution)/shard_map/reshape | solution.py:80
  199.7 16.6 %all-gather.2.cloned.1.call-done = bf16[1,768,6144]{2,1,0:T(8,128)(2,1)} async-done(((bf16[1,48,6144]{2,1,0:T(8,128)(2,1)}), bf16[1,768,6144]{2,1,0:T(8,128)(2,1)}) %all-gather.2.cloned.1.call-update) | async-done | bytes 9437200 | tf_op jit(solution)/shard_map/all_gather | solution.py:84
  216.2 3.4 %fusion.4 = f32[384,768]{1,0:T(8,128)S(1)} fusion(bf16[384,2048]{1,0:T(8,128)(2,1)S(1)} %copy-done.1, bf16[768,6144]{1,0:T(8,128)(2,1)} %bitcast.25), kind=kOutput, calls=%fused_computation.7 | convolution fusion | flops 1207959552 | bytes 5898240 | tf_op jit(solution)/shard_map/dot_general | solution.py:20
  219.7 3.7 %fusion = f32[384,768]{1,0:T(8,128)S(1)} fusion(bf16[384,2048]{1,0:T(8,128)(2,1)S(1)} %copy-done.2, bf16[768,6144]{1,0:T(8,128)(2,1)} %bitcast.26), kind=kOutput, calls=%fused_computation | convolution fusion | flops 1207959552 | bytes 5898240 | tf_op jit(solution)/shard_map/dot_general | solution.py:22
  223.5 4.9 %multiply_reduce_fusion = (bf16[384]{0:T(512)(128)(2,1)S(1)}, f32[384,768]{1,0:T(8,128)}) fusion(f32[384,768]{1,0:T(8,128)S(1)} %fusion, f32[384,768]{1,0:T(8,128)S(1)} %fusion.4, bf16[384,2048]{1,0:T(8,128)(2,1)S(1)} %copy-done.1, bf16[768,6144]{1,0:T(8,128)(2,1)} %bitcast.27), kind=kOutput, calls=%fused_computation.13 | convolution fusion | flops 1210023552 | bytes 8258304 | tf_op jit(solution)/shard_map/dot_general | solution.py:21
  228.4 0.7 convert_element_type.96
  229.1 11.6 %all-to-all-start.4 = ((bf16[32,1,12]{2,1,0:T(2,128)(2,1)}), bf16[32,1,12]{2,1,0:T(2,128)(2,1)S(1)}, u32[]{:S(2)}, u32[]{:S(2)}) async-start(bf16[32,1,12]{2,1,0:T(2,128)(2,1)} %convert_element_type.96), calls=%async_computation.4 | async-start | bytes 32768 | tf_op jit(solution)/shard_map/all_to_all | solution.py:94
  240.8 0.1 copy.38
  240.9 0.1 mul.73
  241.0 9.8 %all-to-all-done.4 = bf16[32,1,12]{2,1,0:T(2,128)(2,1)S(1)} async-done(((bf16[32,1,12]{2,1,0:T(2,128)(2,1)}), bf16[32,1,12]{2,1,0:T(2,128)(2,1)S(1)}, u32[]{:S(2)}, u32[]{:S(2)}) %all-to-all-start.4) | async-done | bytes 800 | tf_op jit(solution)/shard_map/all_to_all | solution.py:94
  250.8 0.1 convert_reduce_fusion.1
  250.8 0.1 reshape.119
  250.9 0.2 select_reduce_fusion
  251.2 0.1 convert_element_type.95
  251.3 13.1 %all_to_all.27 = bf16[32,1,12]{2,1,0:T(2,128)(2,1)S(1)} all-to-all(bf16[32,1,12]{2,1,0:T(2,128)(2,1)S(1)} %convert_element_type.95), channel_id=1, replica_groups=mesh['dp'=2,'ctx'=8,'exp'=32] {'exp'}, dimensions={0} | all-to-all | bytes 1536 | tf_op jit(solution)/shard_map/all_to_all | solution.py:70
  264.4 0.1 convert_reduce_fusion.2
  264.4 0.1 reshape.118
  264.5 4.8 %fusion.2 = f32[384,2048]{1,0:T(8,128)S(1)} fusion(bf16[768,6144]{1,0:T(8,128)(2,1)} %bitcast.28, f32[384,768]{1,0:T(8,128)} %copy-done.5, f32[384,768]{1,0:T(8,128)} %get-tuple-element.13, f32[384,768]{1,0:T(8,128)} %copy-done.7, f32[384]{0:T(512)S(1)} %reshape.118), kind=kOutput, calls=%fused_computation.5 | convolution fusion | flops 1211203584 | bytes 9831936 | tf_op jit(solution)/shard_map/dot_general | solution.py:28
  269.4 3.5 %add_convert_fusion = bf16[384,2048]{1,0:T(8,128)(2,1)S(1)} fusion(f32[384,2048]{1,0:T(8,128)S(1)} %fusion.2, bf16[768,6144]{1,0:T(8,128)(2,1)} %bitcast.29, f32[384,768]{1,0:T(8,128)S(1)} %copy-done.8, f32[384]{0:T(512)S(1)} %reshape.118, f32[384,768]{1,0:T(8,128)S(1)} %copy-done.6), kind=kOutput, calls=%fused_computation.2 | convolution fusion | flops 1211596800 | bytes 10225152 | tf_op jit(solution)/shard_map/dot_general | solution.py:29
  272.9 1.5 reshape.115
  274.4 4.0 %all-to-all-start.3 = ((bf16[32,12,2048]{2,1,0:T(8,128)(2,1)}), bf16[32,12,2048]{2,1,0:T(8,128)(2,1)S(1)}, u32[]{:S(2)}, u32[]{:S(2)}) async-start(bf16[32,12,2048]{2,1,0:T(8,128)(2,1)} %reshape.115), calls=%async_computation.3 | async-start | bytes 4194304 | tf_op jit(solution)/shard_map/all_to_all | solution.py:87
  278.5 0.1 reshape.117
  278.6 0.6 copy.41
  279.2 50.5 %all-to-all-done.3 = bf16[32,12,2048]{2,1,0:T(8,128)(2,1)S(1)} async-done(((bf16[32,12,2048]{2,1,0:T(8,128)(2,1)}), bf16[32,12,2048]{2,1,0:T(8,128)(2,1)S(1)}, u32[]{:S(2)}, u32[]{:S(2)}) %all-to-all-start.3) | async-done | bytes 1572896 | tf_op jit(solution)/shard_map/all_to_all | solution.py:87
  329.8 1.3 reshape.116
  331.1 2.6 convolution_convert_fusion.2
  (21 shorter events, 0.1 us)
Async XLA Ops:
  7.2 3.8 %copy-start = (bf16[128,2048]{1,0:T(8,128)(2,1)S(1)}, bf16[128,2048]{1,0:T(8,128)(2,1)}, u32[]{:S(2)}) copy-start(bf16[128,2048]{1,0:T(8,128)(2,1)} %param.5) | copy-start | bytes 1572868
  7.2 209.1 %all-gather.2.cloned.1.call-start = ((), (), s32[]{:S(2)}) async-start(), calls=%async_computation.5 | async-start | bytes 10027008 | tf_op jit(solution)/shard_map/all_gather | solution.py:84
  13.2 13.1 %copy-start.3 = (bf16[128,2048]{1,0:T(8,128)(2,1)S(1)}, bf16[128,2048]{1,0:T(8,128)(2,1)}, u32[]{:S(2)}) copy-start(bf16[128,2048]{1,0:T(8,128)(2,1)} %param.6) | copy-start | bytes 1572868
  13.2 75.0 %all-to-all-start.2 = ((bf16[32,12,2048]{2,1,0:T(8,128)(2,1)}), bf16[32,12,2048]{2,1,0:T(8,128)(2,1)S(1)}, u32[]{:S(2)}, u32[]{:S(2)}) async-start(bf16[32,12,2048]{2,1,0:T(8,128)(2,1)} %reshape.113), calls=%async_computation.2 | async-start | bytes 4194304 | tf_op jit(solution)/shard_map/all_to_all | solution.py:56
  88.2 107.8 %all-to-all-start.1 = ((bf16[32,12,2048]{2,1,0:T(8,128)(2,1)}), bf16[32,12,2048]{2,1,0:T(8,128)(2,1)}, u32[]{:S(2)}, u32[]{:S(2)}) async-start(bf16[32,12,2048]{2,1,0:T(8,128)(2,1)} %reshape.110), calls=%async_computation.1 | async-start | bytes 4194304 | tf_op jit(solution)/shard_map/all_to_all | solution.py:63
  98.9 117.3 %copy-start.1 = (bf16[384,2048]{1,0:T(8,128)(2,1)S(1)}, bf16[384,2048]{1,0:T(8,128)(2,1)}, u32[]{:S(2)}) copy-start(bf16[384,2048]{1,0:T(8,128)(2,1)} %reshape.114) | copy-start | bytes 4718596
  216.2 3.4 %copy-start.2 = (bf16[384,2048]{1,0:T(8,128)(2,1)S(1)}, bf16[384,2048]{1,0:T(8,128)(2,1)}, u32[]{:S(2)}) copy-start(bf16[384,2048]{1,0:T(8,128)(2,1)} %reshape.111) | copy-start | bytes 4718596
  219.7 3.8 %copy-start.5 = (f32[384,768]{1,0:T(8,128)}, f32[384,768]{1,0:T(8,128)S(1)}, u32[]{:S(2)}) copy-start(f32[384,768]{1,0:T(8,128)S(1)} %fusion.4) | copy-start | bytes 3538948
  223.5 4.9 %copy-start.7 = (f32[384,768]{1,0:T(8,128)}, f32[384,768]{1,0:T(8,128)S(1)}, u32[]{:S(2)}) copy-start(f32[384,768]{1,0:T(8,128)S(1)} %fusion) | copy-start | bytes 3538948
  223.5 17.3 %copy-start.4 = (f32[128,2]{0,1:T(2,128)S(1)}, f32[128,2]{0,1:T(2,128)}, u32[]{:S(2)}) copy-start(f32[128,2]{0,1:T(2,128)} %param.9) | copy-start | bytes 3076
  229.1 21.7 %all-to-all-start.4 = ((bf16[32,1,12]{2,1,0:T(2,128)(2,1)}), bf16[32,1,12]{2,1,0:T(2,128)(2,1)S(1)}, u32[]{:S(2)}, u32[]{:S(2)}) async-start(bf16[32,1,12]{2,1,0:T(2,128)(2,1)} %convert_element_type.96), calls=%async_computation.4 | async-start | bytes 32768 | tf_op jit(solution)/shard_map/all_to_all | solution.py:94
  264.5 4.8 %copy-start.6 = (f32[384,768]{1,0:T(8,128)S(1)}, f32[384,768]{1,0:T(8,128)}, u32[]{:S(2)}) copy-start(f32[384,768]{1,0:T(8,128)} %copy-done.5) | copy-start | bytes 3538948
  264.5 4.8 %copy-start.8 = (f32[384,768]{1,0:T(8,128)S(1)}, f32[384,768]{1,0:T(8,128)}, u32[]{:S(2)}) copy-start(f32[384,768]{1,0:T(8,128)} %copy-done.7) | copy-start | bytes 3538948
  274.4 55.3 %all-to-all-start.3 = ((bf16[32,12,2048]{2,1,0:T(8,128)(2,1)}), bf16[32,12,2048]{2,1,0:T(8,128)(2,1)S(1)}, u32[]{:S(2)}, u32[]{:S(2)}) async-start(bf16[32,12,2048]{2,1,0:T(8,128)(2,1)} %reshape.115), calls=%async_computation.3 | async-start | bytes 4194304 | tf_op jit(solution)/shard_map/all_to_all | solution.py:87
Sparse Core Ops, SparseCore 0:
  11.3 204.8 all-gather.1
where the time goes:
time: 341 us
  waiting for transfers between devices  231 us (68%)
  starting transfers between devices  38.1 us (11%)
  matrix products  25.4 us (7%)
  local copies, waits for them, and re-layouts  16.6 us (5%)
  between operations  14.3 us (4%)
  blocking collectives  13.1 us (4%)
    all_to_all x1, waiting for transfers between devices, body(): lax.all_to_all(dy_slots.reshape(experts, capacity, model_width), 'exp', s...  97.1 us
    all_to_all x1, waiting for transfers between devices, body(): lax.all_to_all(x_slots.reshape(experts, capacity, model_width), 'exp', sp...  56.7 us
    all_to_all x1, waiting for transfers between devices, body(): lax.all_to_all(grad_slots.astype(jnp.bfloat16).reshape(experts, capacity,...  50.5 us
    all_gather x1, waiting for transfers between devices, body(): lax.all_gather(expert_weights, ('dp', 'ctx'), axis=1, tiled=True)  16.6 us
    all_to_all x1, blocking collectives, body(): lax.all_to_all(w_slots.reshape(experts, capacity).astype(jnp.bfloat16), '...  13.1 us
    all_to_all x1, starting transfers between devices, body(): lax.all_to_all(x_slots.reshape(experts, capacity, model_width), 'exp', sp...  13 us
    all_to_all x1, starting transfers between devices, body(): lax.all_to_all(comb_slots.reshape(experts, capacity).astype(jnp.bfloat16)...  11.6 us
    all_to_all x1, waiting for transfers between devices, body(): lax.all_to_all(comb_slots.reshape(experts, capacity).astype(jnp.bfloat16)...  9.77 us
  transfers between devices with their start and end apart: 5, of which 5 were waited for; matrix products, arithmetic and copies ran while one was open for 5% of the time, Pallas kernels for 0%

commit v1 on v0

v1 whole, which is shorter than its diff:
```python
import functools

import jax
import jax.numpy as jnp
from jax import lax
from jax.experimental import pallas as pl
from jax.experimental.pallas import tpu as pltpu
from jax.sharding import PartitionSpec as P

MESH = pl.DeviceIdType.MESH
BF16 = jnp.bfloat16
F32 = jnp.float32
ROWS = 128
CAP = 12
BLOCK = 16
BLOCKS = 32
CHUNKS = 4
NX, NY, NZ = 4, 8, 8
D = 2048
SEND = 3 * D // 2
BACK = 3 * D // 4
DY_TAIL = D // 2
G_TAIL = D // 4
UNITS = 768
SHARD = 48
TILE = 256


def place():
    core = lax.axis_index("dp")
    ctx = lax.axis_index("ctx")
    exp = lax.axis_index("exp")
    return core, ctx % NX, exp % NY, (ctx // NX) * 4 + exp // NY


def device(core, x, y, z):
    return (core, (z // 4) * NX + x, (z % 4) * NY + y)


def partner(me, step_y, step_z):
    core, x, y, z = me
    far = jnp.where(step_z == 2, ((z // 2) % 2 + core) % 2, jnp.where(step_z == 3, 1, 0))
    return device(core, x, (y + step_y) % NY, (z + step_z + 4 * far) % NZ)


def iota(shape, dim):
    return lax.broadcasted_iota(jnp.int32, shape, dim)


def nt(a, b):
    return lax.dot_general(a, b, (((1,), (1,)), ((), ())), preferred_element_type=F32)


def nn(a, b):
    return jnp.dot(a, b, preferred_element_type=F32)


def one(cond):
    return jnp.where(cond, 1.0, 0.0).astype(BF16)


def kernel(
    tok, cot, w_ref, rid, cmb, out, gcomb,
    wb, xs, xr, gs, gr, tail, acc, home, cs, cr, vx, vxt,
    local_sem, w_send, w_recv, x_send, x_recv, g_send, g_recv, c_send, c_recv,
):
    me = place()
    core, x, y, z = me
    barrier = pltpu.get_barrier_semaphore()

    def greet(k, carry):
        pl.semaphore_signal(
            barrier, inc=1, device_id=partner(me, k % NY, k // NY), device_id_type=MESH
        )
        return carry

    lax.fori_loop(1, BLOCKS, greet, 0)
    z_far = device(core, x, y, (z + 4) % NZ)
    x_up = device(core, (x + 1) % NX, y, z)
    x_down = device(core, (x + 3) % NX, y, z)
    twin = device(1 - core, x, y, z)
    for other in (z_far, x_up, x_down, twin):
        pl.semaphore_signal(barrier, inc=1, device_id=other, device_id_type=MESH)

    def shard(half, side, step):
        return wb.at[pl.ds((half * 8 + side * 4 + step) * SHARD, SHARD), :]

    own_copy = pltpu.make_async_copy(w_ref, shard(0, 0, 0), local_sem.at[0])
    own_copy.start()

    ids = rid[...]
    rel = ((ids // NY - z % 4 + 4) % 4) * NY + (ids % NY - y + NY) % NY
    first, second = rel[:, 0:1], rel[:, 1:2]
    lane = iota((ROWS, ROWS), 1)
    sub = iota((ROWS, ROWS), 0)
    named = (first == lane) | (second == lane)
    ordinal = nn(one(lane < sub), one(named))
    val = jnp.where(named, ordinal, -1.0).astype(BF16)
    slots = BLOCKS * BLOCK
    spread = one(iota((slots, ROWS), 0) // BLOCK == iota((slots, ROWS), 1))
    vxt[...] = nt(spread, val)
    vx[...] = nt(val, spread)

    pl.semaphore_wait(barrier, BLOCKS - 1 + 4)

    def send_w(n, src, dst, target):
        copy = pltpu.make_async_remote_copy(
            src_ref=src, dst_ref=dst, send_sem=w_send.at[n], recv_sem=w_recv.at[n],
            device_id=target, device_id_type=MESH,
        )
        copy.start()
        return copy

    z_copy = send_w(0, w_ref, shard(1, 0, 0), z_far)
    up0 = send_w(1, w_ref, shard(0, 0, 1), x_up)
    down0 = send_w(2, w_ref, shard(0, 0, 3), x_down)
    twin00 = send_w(3, w_ref, shard(0, 1, 0), twin)

    def x_copy(k):
        rows = pl.ds(pl.multiple_of(k * BLOCK, BLOCK), BLOCK)
        return pltpu.make_async_remote_copy(
            src_ref=xs.at[rows, :], dst_ref=xr.at[rows, :],
            send_sem=x_send.at[k], recv_sem=x_recv.at[k],
            device_id=partner(me, k % NY, k // NY), device_id_type=MESH,
        )

    def g_copy(k):
        rows = pl.ds(pl.multiple_of(k * BLOCK, BLOCK), BLOCK)
        return pltpu.make_async_remote_copy(
            src_ref=gs.at[rows, :], dst_ref=gr.at[rows, :],
            send_sem=g_send.at[k], recv_sem=g_recv.at[k],
            device_id=partner(me, (NY - k % NY) % NY, (4 - k // NY) % 4), device_id_type=MESH,
        )

    def c_copy(k):
        return pltpu.make_async_remote_copy(
            src_ref=cs.at[k // NY], dst_ref=cr.at[k],
            send_sem=c_send.at[k], recv_sem=c_recv.at[k],
            device_id=partner(me, (NY - k % NY) % NY, (4 - k // NY) % 4), device_id_type=MESH,
        )

    def each(chunk, act):
        def step(i, carry):
            act(chunk * 8 + i)
            return carry
        lax.fori_loop(jnp.where(chunk == 0, 1, 0), 8, step, 0)

    def dispatch(chunk, carry):
        rows = pl.ds(pl.multiple_of(chunk * ROWS, ROWS), ROWS)
        v = vxt[rows, :].astype(jnp.int32)
        row = sub % BLOCK
        put = one((v == row) & (row < CAP))
        ends = cot[:, DY_TAIL:]
        pieces = (tok[:, :DY_TAIL], tok[:, DY_TAIL:], cot[:, :DY_TAIL])
        for j, piece in enumerate(pieces):
            put_end = one((v == 3 * (row - CAP) + j) & (row >= CAP))
            got = nn(put, piece) + nn(put_end, ends)
            xs[rows, j * DY_TAIL : (j + 1) * DY_TAIL] = got.astype(BF16)
        each(chunk, lambda k: x_copy(k).start())
        return carry

    lax.fori_loop(0, CHUNKS, dispatch, 0)
    xr[0:BLOCK, :] = xs[0:BLOCK, :]

    started = [z_copy, up0, down0, twin00]

    def pass_on(n, half, step, target, to_step, side=0):
        started.append(send_w(n, shard(half, 0, step), shard(half, side, to_step), target))

    up0.wait_recv()
    pass_on(4, 0, 1, x_up, 2)
    pass_on(5, 0, 1, twin, 1, side=1)
    down0.wait_recv()
    pass_on(6, 0, 3, twin, 3, side=1)
    z_copy.wait_recv()
    pass_on(7, 1, 0, x_up, 1)
    pass_on(8, 1, 0, x_down, 3)
    pass_on(9, 1, 0, twin, 0, side=1)
    started[4].wait_recv()
    pass_on(10, 0, 2, twin, 2, side=1)
    started[8].wait_recv()
    pass_on(11, 1, 3, x_down, 2)
    pass_on(12, 1, 3, twin, 3, side=1)
    started[7].wait_recv()
    pass_on(13, 1, 1, twin, 1, side=1)
    started[11].wait_recv()
    pass_on(14, 1, 2, twin, 2, side=1)
    for n in (3, 5, 6, 9, 10, 12, 13, 14):
        started[n].wait_recv()
    own_copy.wait()

    row = sub % BLOCK
    col = lane % BLOCK
    same = sub // BLOCK == lane // BLOCK

    def work(chunk, carry):
        each(chunk, lambda k: x_copy(k).wait_recv())
        rows = pl.ds(pl.multiple_of(chunk * ROWS, ROWS), ROWS)
        end = jnp.zeros((ROWS, DY_TAIL), F32)
        for j in range(3):
            take = one(same & (col >= CAP) & (row == 3 * (col - CAP) + j))
            end = end + nn(take, xr[rows, j * DY_TAIL : (j + 1) * DY_TAIL])
        tail[...] = end.astype(BF16)

        def units(t, total):
            us = pl.ds(pl.multiple_of(t * TILE, TILE), TILE)
            xv = xr[rows, 0:D]
            gate = nt(xv, wb[us, 0:D])
            up = nt(xv, wb[us, D : 2 * D])
            back = nt(xr[rows, D : D + DY_TAIL], wb[us, 2 * D : 2 * D + DY_TAIL])
            back = back + nt(tail[...], wb[us, 2 * D + DY_TAIL : 3 * D])
            sig = jax.nn.sigmoid(gate)
            act = gate * sig
            d_up = back * act
            d_gate = back * up * (sig * (1.0 + gate * (1.0 - sig)))
            got = nn(d_gate.astype(BF16), wb[us, 0:D]) + nn(d_up.astype(BF16), wb[us, D : 2 * D])

            @pl.when(t == 0)
            def _():
                acc[...] = got

            @pl.when(t > 0)
            def _():
                acc[...] += got

            return total + jnp.sum(d_up * up, axis=1, keepdims=True)

        total = lax.fori_loop(0, UNITS // TILE, units, jnp.zeros((ROWS, 1), F32))
        cs[chunk] = jnp.transpose(jnp.broadcast_to(total, (ROWS, ROWS)))[0:1, :]
        ends = acc[:, BACK:D].astype(BF16)
        for j in range(3):
            cols = slice(j * G_TAIL, (j + 1) * G_TAIL)
            take = one(same & (row >= CAP) & (col == 3 * (row - CAP) + j))
            moved = nn(take, ends)
            keep = iota((ROWS, G_TAIL), 0) % BLOCK < CAP
            gs[rows, cols] = jnp.where(keep, acc[:, cols], moved).astype(BF16)

        def give(k):
            g_copy(k).start()
            c_copy(k).start()

        each(chunk, give)
        return carry

    lax.fori_loop(0, CHUNKS, work, 0)
    gr[0:BLOCK, :] = gs[0:BLOCK, :]
    cr[0] = cs[0]

    c0, c1 = cmb[:, 0:1], cmb[:, 1:2]

    def gather(chunk, carry):
        each(chunk, lambda k: (g_copy(k).wait_recv(), c_copy(k).wait_recv()))
        rows = pl.ds(pl.multiple_of(chunk * ROWS, ROWS), ROWS)
        v = vx[:, rows].astype(jnp.int32)
        block = chunk * 8 + lane // BLOCK
        at0, at1 = first == block, second == block
        hit = (v == col) & (col < CAP)
        hit0, hit1 = hit & at0, hit & at1
        end = jnp.zeros((ROWS, G_TAIL), F32)
        for j in range(3):
            cols = slice(j * G_TAIL, (j + 1) * G_TAIL)
            part = gr[rows, cols]
            got = c0 * nn(one(hit0), part) + c1 * nn(one(hit1), part)
            hit_end = (v == 3 * (col - CAP) + j) & (col >= CAP)
            end = end + c0 * nn(one(hit_end & at0), part) + c1 * nn(one(hit_end & at1), part)

            @pl.when(chunk == 0)
            def _():
                home[:, cols] = got

            @pl.when(chunk > 0)
            def _():
                home[:, cols] += got

        @pl.when(chunk == 0)
        def _():
            home[:, BACK:D] = end

        @pl.when(chunk > 0)
        def _():
            home[:, BACK:D] += end

        line = jnp.zeros((1, ROWS), F32)
        for i in range(8):
            line = jnp.where(iota((1, ROWS), 1) // BLOCK == i, cr[chunk * 8 + i], line)
        g0, g1 = carry
        g0 = g0 + jnp.sum(jnp.where(hit0, line, 0.0), axis=1, keepdims=True)
        g1 = g1 + jnp.sum(jnp.where(hit1, line, 0.0), axis=1, keepdims=True)
        return g0, g1

    zero = jnp.zeros((ROWS, 1), F32)
    g0, g1 = lax.fori_loop(0, CHUNKS, gather, (zero, zero))
    out[...] = home[...].astype(BF16)
    gcomb[...] = jnp.where(iota((ROWS, 2), 1) == 0, g0, g1)

    def finish(k, carry):
        x_copy(k).wait_send()
        g_copy(k).wait_send()
        c_copy(k).wait_send()
        return carry

    lax.fori_loop(1, BLOCKS, finish, 0)
    for copy in started:
        copy.wait_send()


def body(tokens, cotangent, expert_weights, route_ids, combine):
    vmem = pl.BlockSpec(memory_space=pltpu.VMEM)
    slots = BLOCKS * BLOCK
    dma = pltpu.SemaphoreType.DMA
    return pl.pallas_call(
        kernel,
        out_shape=(
            jax.ShapeDtypeStruct((ROWS, D), BF16),
            jax.ShapeDtypeStruct((ROWS, 2), F32),
        ),
        in_specs=[vmem, vmem, pl.BlockSpec(memory_space=pl.ANY), vmem, vmem],
        out_specs=(vmem, vmem),
        scratch_shapes=[
            pltpu.VMEM((UNITS, 3 * D), BF16),
            pltpu.VMEM((slots, SEND), BF16),
            pltpu.VMEM((slots, SEND), BF16),
            pltpu.VMEM((slots, BACK), BF16),
            pltpu.VMEM((slots, BACK), BF16),
            pltpu.VMEM((ROWS, DY_TAIL), BF16),
            pltpu.VMEM((ROWS, D), F32),
            pltpu.VMEM((ROWS, D), F32),
            pltpu.VMEM((CHUNKS, 1, ROWS), F32),
            pltpu.VMEM((BLOCKS, 1, ROWS), F32),
            pltpu.VMEM((ROWS, slots), F32),
            pltpu.VMEM((slots, ROWS), F32),
            dma((1,)),
            dma((15,)), dma((15,)),
            dma((BLOCKS,)), dma((BLOCKS,)),
            dma((BLOCKS,)), dma((BLOCKS,)),
            dma((BLOCKS,)), dma((BLOCKS,)),
        ],
        compiler_params=pltpu.CompilerParams(
            collective_id=0, has_side_effects=True, vmem_limit_bytes=48 << 20
        ),
        cost_estimate=pl.CostEstimate(flops=8 << 30, bytes_accessed=4 << 20, transcendentals=1 << 20),
    )(tokens, cotangent, expert_weights[0], route_ids, combine)


def solution(mesh):
    rows = P(("dp", "ctx", "exp"), None)
    return jax.shard_map(
        body,
        mesh=mesh,
        in_specs=(rows, rows, P("exp", ("dp", "ctx"), None), rows, rows),
        out_specs=(rows, rows),
        check_vma=False,
    )
```

time: 341 us -> 158 us (0.46)
  the two profiles are of different devices: /device:TPU:2 before, /device:TPU:233 now
where the time goes in v1:
time: 158 us
  Pallas kernels  151 us (96%)
  local copies, waits for them, and re-layouts  6.03 us (4%)
    pallas_call x1, Pallas kernels, body(): pl.pallas_call(kernel, out_shape=(jax.ShapeDtypeStruct((ROWS, D), BF16),...  151 us
    unnamed x13, local copies, waits for them, and re-layouts  5.4 us

profile of v1, /device:TPU:233, one launch (start us, length us, event | category | flops | bytes accessed | tf_op | source)
XLA Modules:
  0.0 157.9 jit_solution(1589975214813624549)
XLA Ops:
  0.6 0.0 copy-start.3
  0.6 0.7 copy-done.3
  1.3 0.0 copy-start.4
  1.3 0.1 copy.7.rid
  1.4 0.6 copy-done.4
  2.0 0.1 copy.8.cmb
  2.1 0.0 copy-start
  2.1 1.1 copy-done
  3.2 0.0 copy-start.1
  3.2 1.0 copy-done.1
  4.2 0.0 copy-start.2
  4.2 1.0 copy-done.2
  5.3 151.2 %shard_map.68 = (bf16[128,2048]{1,0:T(8,128)(2,1)S(1)}, f32[128,2]{1,0:T(8,128)S(1)}) custom-call(bf16[128,2048]{1,0:T(8,128)(2,1)S(1)} %copy-done.1, bf16[128,2048]{1,0:T(8,128)(2,1)S(1)} %copy-done.2, bf16[48,6144]{1,0:T(8,128)(2,1)S(1)} %bitcast.1, s32[128,2]{1,0:T(8,128)S(1)} %copy.7.rid, f32[128,2]{1,0:T(8,128)S(1)} %copy.8.cmb), custom_call_target="tpu_custom_call" | custom-call | flops 8589934592 | bytes 4194304 | tf_op jit(solution)/shard_map/pallas_call | solution.py:311
  156.4 0.6 copy.9
  157.1 0.8 copy.11
Async XLA Ops:
  0.6 0.7 copy-start.3
  1.3 0.7 copy-start.4
  2.1 1.1 copy-start
  3.2 1.0 copy-start.1
  4.2 1.0 copy-start.2

commit v2 on v1

v2 whole, which is shorter than its diff:
```python
import functools

import jax
import jax.numpy as jnp
from jax import lax
from jax.experimental import pallas as pl
from jax.experimental.pallas import tpu as pltpu
from jax.sharding import PartitionSpec as P

MESH = pl.DeviceIdType.MESH
BF16 = jnp.bfloat16
F32 = jnp.float32
ROWS = 128
CAP = 12
BLOCK = 16
BLOCKS = 32
GROUPS = 4
WIDE = 256
NX, NY, NZ = 4, 8, 8
D = 2048
SEND = 3 * D // 2
BACK = 3 * D // 4
DY_TAIL = D // 2
G_TAIL = D // 4
UNITS = 768
SHARD = 48
PIECE = 16
W_COPIES = 31
TILE = 256


def place():
    core = lax.axis_index("dp")
    ctx = lax.axis_index("ctx")
    exp = lax.axis_index("exp")
    return core, ctx % NX, exp % NY, (ctx // NX) * 4 + exp // NY


def device(core, x, y, z):
    return (core, (z // 4) * NX + x, (z % 4) * NY + y)


def partner(me, step_y, step_z):
    core, x, y, z = me
    far = jnp.where(step_z == 2, ((z // 2) % 2 + core) % 2, jnp.where(step_z == 3, 1, 0))
    return device(core, x, (y + step_y) % NY, (z + step_z + 4 * far) % NZ)


def step_of(group):
    return jnp.where(group < 2, group, 5 - group)


def iota(shape, dim):
    return lax.broadcasted_iota(jnp.int32, shape, dim)


def nt(a, b):
    return lax.dot_general(a, b, (((1,), (1,)), ((), ())), preferred_element_type=F32)


def nn(a, b):
    return jnp.dot(a, b, preferred_element_type=F32)


def one(cond):
    return jnp.where(cond, 1.0, 0.0).astype(BF16)


def kernel(
    tok_hbm, cot_hbm, w_ref, rid_hbm, cmb_hbm, out, gcomb,
    tok, cot, rid, cmb, wb, xs, xr, gs, gr, tail, ends, dgs, dus, home, cs, cr, vx, vxt,
    local_sem, w_send, w_recv, x_send, x_recv, g_send, g_recv, c_send, c_recv,
):
    me = place()
    core, x, y, z = me
    barrier = pltpu.get_barrier_semaphore()

    def greet(k, carry):
        pl.semaphore_signal(
            barrier, inc=1, device_id=partner(me, k % NY, step_of(k // NY)), device_id_type=MESH
        )
        return carry

    lax.fori_loop(1, BLOCKS, greet, 0)
    z_far = device(core, x, y, (z + 4) % NZ)
    x_up = device(core, (x + 1) % NX, y, z)
    x_down = device(core, (x + 3) % NX, y, z)
    twin = device(1 - core, x, y, z)
    for other in (z_far, x_up, x_down, twin):
        pl.semaphore_signal(barrier, inc=1, device_id=other, device_id_type=MESH)

    def shard(half, side, step, piece=None):
        at = (half * 8 + side * 4 + step) * SHARD
        if piece is None:
            return wb.at[pl.ds(at, SHARD), :]
        return wb.at[pl.ds(at + piece * PIECE, PIECE), :]

    loads = []
    for n, (src, dst) in enumerate(
        ((rid_hbm, rid), (tok_hbm, tok), (cot_hbm, cot), (cmb_hbm, cmb), (w_ref, shard(0, 0, 0)))
    ):
        load = pltpu.make_async_copy(src, dst, local_sem.at[n])
        load.start()
        loads.append(load)
    loads[0].wait()

    ids = rid[...]
    step_z = (ids // NY - z % 4 + 4) % 4
    rel = (step_of(step_z) * NY + (ids % NY - y + NY) % NY).astype(F32)

    def column(line):
        return jnp.transpose(jnp.broadcast_to(line, (ROWS, ROWS)))

    first = column(rel[0:1, :]).astype(jnp.int32)
    second = column(rel[1:2, :]).astype(jnp.int32)
    lane = iota((ROWS, ROWS), 1)
    sub = iota((ROWS, ROWS), 0)
    named = (first == lane) | (second == lane)
    ordinal = nn(one(lane < sub), one(named))
    val = jnp.where(named, ordinal, -1.0).astype(BF16)
    slots = BLOCKS * BLOCK
    spread = one(iota((slots, ROWS), 0) // BLOCK == iota((slots, ROWS), 1))
    vxt[...] = nt(spread, val)
    vx[...] = nt(val, spread)

    pl.semaphore_wait(barrier, BLOCKS - 1 + 4)

    started = []

    def send_w(src, dst, target):
        n = len(started)
        copy = pltpu.make_async_remote_copy(
            src_ref=src, dst_ref=dst, send_sem=w_send.at[n], recv_sem=w_recv.at[n],
            device_id=target, device_id_type=MESH,
        )
        copy.start()
        started.append(copy)
        return copy

    pieces = range(SHARD // PIECE)
    z_in = [
        send_w(w_ref.at[pl.ds(p * PIECE, PIECE), :], shard(1, 0, 0, p), z_far) for p in pieces
    ]
    up0 = send_w(w_ref, shard(0, 0, 1), x_up)
    down0 = send_w(w_ref, shard(0, 0, 3), x_down)
    twins = [send_w(w_ref, shard(0, 1, 0), twin)]

    def x_copy(k):
        rows = pl.ds(pl.multiple_of(k * BLOCK, BLOCK), BLOCK)
        return pltpu.make_async_remote_copy(
            src_ref=xs.at[rows, :], dst_ref=xr.at[rows, :],
            send_sem=x_send.at[k], recv_sem=x_recv.at[k],
            device_id=partner(me, k % NY, step_of(k // NY)), device_id_type=MESH,
        )

    def source(k):
        return partner(me, (NY - k % NY) % NY, (4 - step_of(k // NY)) % 4)

    def g_copy(k):
        rows = pl.ds(pl.multiple_of(k * BLOCK, BLOCK), BLOCK)
        return pltpu.make_async_remote_copy(
            src_ref=gs.at[rows, :], dst_ref=gr.at[rows, :],
            send_sem=g_send.at[k], recv_sem=g_recv.at[k],
            device_id=source(k), device_id_type=MESH,
        )

    def c_copy(k):
        return pltpu.make_async_remote_copy(
            src_ref=cs.at[k // NY], dst_ref=cr.at[k],
            send_sem=c_send.at[k], recv_sem=c_recv.at[k],
            device_id=source(k), device_id_type=MESH,
        )

    def loop(low, high, act):
        def step(i, carry):
            act(i)
            return carry
        lax.fori_loop(low, high, step, 0)

    loads[1].wait()
    loads[2].wait()

    def dispatch(group):
        rows = pl.ds(pl.multiple_of(group * ROWS, ROWS), ROWS)
        v = vxt[rows, :].astype(jnp.int32)
        row = sub % BLOCK
        put = one((v == row) & (row < CAP))
        parts = (tok[:, :DY_TAIL], tok[:, DY_TAIL:], cot[:, :DY_TAIL])
        for j, part in enumerate(parts):
            put_end = one((v == 3 * (row - CAP) + j) & (row >= CAP))
            got = nn(put, part) + nn(put_end, cot[:, DY_TAIL:])
            xs[rows, j * DY_TAIL : (j + 1) * DY_TAIL] = got.astype(BF16)

    dispatch(0)
    loop(1, 8, lambda k: x_copy(k).start())
    loop(1, 3, dispatch)

    def two(i):
        x_copy(8 + i).start()
        x_copy(16 + (i + 4) % 8).start()

    loop(0, 8, two)
    dispatch(3)
    loop(24, 32, lambda k: x_copy(k).start())
    xr[0:BLOCK, :] = xs[0:BLOCK, :]

    up, down, across = [], [], []

    def to_twin(half, step, piece=None):
        twins.append(send_w(shard(half, 0, step, piece), shard(half, 1, step, piece), twin))

    def from_z(p):
        z_in[p].wait_recv()
        up.append(send_w(shard(1, 0, 0, p), shard(1, 0, 1, p), x_up))
        down.append(send_w(shard(1, 0, 0, p), shard(1, 0, 3, p), x_down))
        to_twin(1, 0, p)

    def from_x(p):
        down[p].wait_recv()
        across.append(send_w(shard(1, 0, 3, p), shard(1, 0, 2, p), x_down))
        to_twin(1, 3, p)
        up[p].wait_recv()
        to_twin(1, 1, p)

    def from_across(p):
        across[p].wait_recv()
        to_twin(1, 2, p)

    up0.wait_recv()
    across0 = send_w(shard(0, 0, 1), shard(0, 0, 2), x_up)
    to_twin(0, 1)
    down0.wait_recv()
    to_twin(0, 3)
    from_z(0)
    across0.wait_recv()
    to_twin(0, 2)
    from_z(1)
    from_x(0)
    from_z(2)
    from_x(1)
    from_across(0)
    from_x(2)
    from_across(1)
    from_across(2)
    for copy in twins:
        copy.wait_recv()
    loads[4].wait()

    sub2 = iota((WIDE, WIDE), 0)
    lane2 = iota((WIDE, WIDE), 1)
    row2 = sub2 % BLOCK
    col2 = lane2 % BLOCK
    same2 = sub2 // BLOCK == lane2 // BLOCK

    def work(chunk):
        loop(jnp.where(chunk == 0, 1, 16), 16 + 16 * chunk, lambda k: x_copy(k).wait_recv())
        rows = pl.ds(pl.multiple_of(chunk * WIDE, WIDE), WIDE)
        end = jnp.zeros((WIDE, DY_TAIL), F32)
        for j in range(3):
            take = one(same2 & (col2 >= CAP) & (row2 == 3 * (col2 - CAP) + j))
            end = end + nn(take, xr[rows, j * DY_TAIL : (j + 1) * DY_TAIL])
        tail[...] = end.astype(BF16)

        def units(t, total):
            us = pl.ds(pl.multiple_of(t * TILE, TILE), TILE)
            xv = xr[rows, 0:D]
            gate = nt(xv, wb[us, 0:D])
            up_pre = nt(xv, wb[us, D : 2 * D])
            back = nt(xr[rows, D : D + DY_TAIL], wb[us, 2 * D : 2 * D + DY_TAIL])
            back = back + nt(tail[...], wb[us, 2 * D + DY_TAIL : 3 * D])
            sig = jax.nn.sigmoid(gate)
            act = gate * sig
            d_up = back * act
            d_gate = back * up_pre * (sig * (1.0 + gate * (1.0 - sig)))
            dgs[:, us] = d_gate.astype(BF16)
            dus[:, us] = d_up.astype(BF16)
            return total + jnp.sum(d_up * up_pre, axis=1, keepdims=True)

        total = lax.fori_loop(0, UNITS // TILE, units, jnp.zeros((WIDE, 1), F32))
        for h in range(2):
            part = jnp.broadcast_to(total[h * ROWS : (h + 1) * ROWS, :], (ROWS, ROWS))
            cs[chunk * 2 + h] = jnp.transpose(part)[0:1, :]

        def grad(low):
            high = low + G_TAIL
            return nn(dgs[...], wb[:, low:high]) + nn(dus[...], wb[:, D + low : D + high])

        ends[...] = grad(BACK).astype(BF16)
        for j in range(3):
            take = one(same2 & (row2 >= CAP) & (col2 == 3 * (row2 - CAP) + j))
            moved = nn(take, ends[...])
            keep = iota((WIDE, G_TAIL), 0) % BLOCK < CAP
            both = jnp.where(keep, grad(j * G_TAIL), moved).astype(BF16)
            gs[rows, j * G_TAIL : (j + 1) * G_TAIL] = both

        def give(i):
            for k in (chunk * 16 + i, chunk * 16 + 8 + (i + 4) % 8):
                @pl.when(k > 0)
                def _():
                    g_copy(k).start()
                    c_copy(k).start()

        loop(0, 8, give)

    loop(0, 2, work)
    gr[0:BLOCK, :] = gs[0:BLOCK, :]
    cr[0] = cs[0]

    loads[3].wait()
    c0, c1 = column(cmb[0:1, :])[:, 0:1], column(cmb[1:2, :])[:, 0:1]
    col = lane % BLOCK

    def gather(group, carry):
        def arrived(k):
            g_copy(k).wait_recv()
            c_copy(k).wait_recv()

        loop(jnp.where(group == 0, 1, group * 8), group * 8 + 8, arrived)
        rows = pl.ds(pl.multiple_of(group * ROWS, ROWS), ROWS)
        v = vx[:, rows].astype(jnp.int32)
        block = group * 8 + lane // BLOCK
        at0, at1 = first == block, second == block
        hit = (v == col) & (col < CAP)
        hit0, hit1 = hit & at0, hit & at1
        end = jnp.zeros((ROWS, G_TAIL), F32)
        for j in range(3):
            cols = slice(j * G_TAIL, (j + 1) * G_TAIL)
            part = gr[rows, cols]
            got = c0 * nn(one(hit0), part) + c1 * nn(one(hit1), part)
            hit_end = (v == 3 * (col - CAP) + j) & (col >= CAP)
            end = end + c0 * nn(one(hit_end & at0), part) + c1 * nn(one(hit_end & at1), part)

            @pl.when(group == 0)
            def _():
                home[:, cols] = got

            @pl.when(group > 0)
            def _():
                home[:, cols] += got

        @pl.when(group == 0)
        def _():
            home[:, BACK:D] = end

        @pl.when(group > 0)
        def _():
            home[:, BACK:D] += end

        line = jnp.zeros((1, ROWS), F32)
        for i in range(8):
            line = jnp.where(iota((1, ROWS), 1) // BLOCK == i, cr[group * 8 + i], line)
        g0, g1 = carry
        g0 = g0 + jnp.sum(jnp.where(hit0, line, 0.0), axis=1, keepdims=True)
        g1 = g1 + jnp.sum(jnp.where(hit1, line, 0.0), axis=1, keepdims=True)
        return g0, g1

    zero = jnp.zeros((ROWS, 1), F32)
    g0, g1 = lax.fori_loop(0, GROUPS, gather, (zero, zero))
    out[...] = home[...].astype(BF16)
    gcomb[0:1, :] = jnp.transpose(jnp.broadcast_to(g0, (ROWS, ROWS)))[0:1, :]
    gcomb[1:2, :] = jnp.transpose(jnp.broadcast_to(g1, (ROWS, ROWS)))[0:1, :]

    def finish(k):
        x_copy(k).wait_send()
        g_copy(k).wait_send()
        c_copy(k).wait_send()

    loop(1, BLOCKS, finish)
    for copy in started:
        copy.wait_send()


def body(tokens, cotangent, expert_weights, route_ids, combine):
    vmem = pl.BlockSpec(memory_space=pltpu.VMEM)
    hbm = pl.BlockSpec(memory_space=pltpu.HBM)
    slots = BLOCKS * BLOCK
    dma = pltpu.SemaphoreType.DMA
    grad_tokens, grad_combine = pl.pallas_call(
        kernel,
        out_shape=(
            jax.ShapeDtypeStruct((ROWS, D), BF16),
            jax.ShapeDtypeStruct((2, ROWS), F32),
        ),
        in_specs=[hbm] * 5,
        out_specs=(vmem, vmem),
        scratch_shapes=[
            pltpu.VMEM((ROWS, D), BF16),
            pltpu.VMEM((ROWS, D), BF16),
            pltpu.VMEM((2, ROWS), jnp.int32),
            pltpu.VMEM((2, ROWS), F32),
            pltpu.VMEM((UNITS, 3 * D), BF16),
            pltpu.VMEM((slots, SEND), BF16),
            pltpu.VMEM((slots, SEND), BF16),
            pltpu.VMEM((slots, BACK), BF16),
            pltpu.VMEM((slots, BACK), BF16),
            pltpu.VMEM((WIDE, DY_TAIL), BF16),
            pltpu.VMEM((WIDE, G_TAIL), BF16),
            pltpu.VMEM((WIDE, UNITS), BF16),
            pltpu.VMEM((WIDE, UNITS), BF16),
            pltpu.VMEM((ROWS, D), F32),
            pltpu.VMEM((GROUPS, 1, ROWS), F32),
            pltpu.VMEM((BLOCKS, 1, ROWS), F32),
            pltpu.VMEM((ROWS, slots), F32),
            pltpu.VMEM((slots, ROWS), F32),
            dma((5,)),
            dma((W_COPIES,)), dma((W_COPIES,)),
            dma((BLOCKS,)), dma((BLOCKS,)),
            dma((BLOCKS,)), dma((BLOCKS,)),
            dma((BLOCKS,)), dma((BLOCKS,)),
        ],
        compiler_params=pltpu.CompilerParams(
            collective_id=0, has_side_effects=True, vmem_limit_bytes=56 << 20
        ),
        cost_estimate=pl.CostEstimate(flops=8 << 30, bytes_accessed=4 << 20, transcendentals=1 << 20),
    )(tokens, cotangent, expert_weights[0], route_ids.T, combine.T)
    return grad_tokens, grad_combine.T


def solution(mesh):
    rows = P(("dp", "ctx", "exp"), None)
    return jax.shard_map(
        body,
        mesh=mesh,
        in_specs=(rows, rows, P("exp", ("dp", "ctx"), None), rows, rows),
        out_specs=(rows, rows),
        check_vma=False,
    )
```

time: 158 us -> 129 us (0.82)
  the two profiles are of different devices: /device:TPU:233 before, /device:TPU:5 now
where the time goes in v2:
time: 129 us; the launch traced here: 128 us
  Pallas kernels  125 us (97%)
  local copies, waits for them, and re-layouts  2.45 us (2%)
    pallas_call x1, Pallas kernels, body(): pl.pallas_call(kernel, out_shape=(jax.ShapeDtypeStruct((ROWS, D), BF16),...  125 us

profile of v2, /device:TPU:5, one launch (start us, length us, event | category | flops | bytes accessed | tf_op | source)
XLA Modules:
  0.0 127.9 jit_solution(9578887307178439379)
XLA Ops:
  0.6 124.8 %shard_map.68 = (bf16[128,2048]{1,0:T(8,128)(2,1)}, f32[2,128]{1,0:T(2,128)}) custom-call(bf16[128,2048]{1,0:T(8,128)(2,1)} %tok_hbm.1, bf16[128,2048]{1,0:T(8,128)(2,1)} %cot_hbm.1, bf16[48,6144]{1,0:T(8,128)(2,1)} %bitcast.5, s32[2,128]{1,0:T(2,128)} %bitcast.6, f32[2,128]{1,0:T(2,128)} %bitcast.7), custom_call_target="tpu_custom_call" | custom-call | flops 8589934592 | bytes 4194304 | tf_op jit(solution)/shard_map/pallas_call | solution.py:378
  125.5 0.0 copy-start
  125.5 1.9 %copy.9 = bf16[128,2048]{1,0:T(8,128)(2,1)} copy(bf16[128,2048]{1,0:T(8,128)(2,1)} %get-tuple-element.8) | data formatting | bytes 1048576
  127.4 0.0 copy-done
  127.4 0.6 copy.10
Async XLA Ops:
  125.5 1.9 %copy-start = (f32[2,128]{1,0:T(2,128)S(1)}, f32[2,128]{1,0:T(2,128)}, u32[]{:S(2)}) copy-start(f32[2,128]{1,0:T(2,128)} %get-tuple-element.5) | copy-start | bytes 3076

commit v3 on v2

--- a/solution.py
+++ b/solution.py
@@ -46,8 +46,15 @@
     return device(core, x, (y + step_y) % NY, (z + step_z + 4 * far) % NZ)
 
 
-def step_of(group):
-    return jnp.where(group < 2, group, 5 - group)
+def table(index, values):
+    found = jnp.full_like(index, values[0])
+    for i, value in enumerate(values[1:]):
+        found = jnp.where(index == i + 1, value, found)
+    return found
+
+
+def steps(k):
+    return table(k // 4, (0, 4, 3, 5, 1, 7, 2, 6)), k % 4
 
 
 def iota(shape, dim):
@@ -77,7 +84,7 @@
 
     def greet(k, carry):
         pl.semaphore_signal(
-            barrier, inc=1, device_id=partner(me, k % NY, step_of(k // NY)), device_id_type=MESH
+            barrier, inc=1, device_id=partner(me, *steps(k)), device_id_type=MESH
         )
         return carry
 
@@ -106,7 +113,8 @@
 
     ids = rid[...]
     step_z = (ids // NY - z % 4 + 4) % 4
-    rel = (step_of(step_z) * NY + (ids % NY - y + NY) % NY).astype(F32)
+    step_y = (ids % NY - y + NY) % NY
+    rel = (table(step_y, (0, 4, 6, 2, 1, 3, 7, 5)) * 4 + step_z).astype(F32)
 
     def column(line):
         return jnp.transpose(jnp.broadcast_to(line, (ROWS, ROWS)))
@@ -150,11 +158,12 @@
         return pltpu.make_async_remote_copy(
             src_ref=xs.at[rows, :], dst_ref=xr.at[rows, :],
             send_sem=x_send.at[k], recv_sem=x_recv.at[k],
-            device_id=partner(me, k % NY, step_of(k // NY)), device_id_type=MESH,
+            device_id=partner(me, *steps(k)), device_id_type=MESH,
         )
 
     def source(k):
-        return partner(me, (NY - k % NY) % NY, (4 - step_of(k // NY)) % 4)
+        step_y, step_z = steps(k)
+        return partner(me, (NY - step_y) % NY, (4 - step_z) % 4)
 
     def g_copy(k):
         rows = pl.ds(pl.multiple_of(k * BLOCK, BLOCK), BLOCK)
@@ -166,7 +175,7 @@
 
     def c_copy(k):
         return pltpu.make_async_remote_copy(
-            src_ref=cs.at[k // NY], dst_ref=cr.at[k],
+            src_ref=cs.at[k // 8], dst_ref=cr.at[k],
             send_sem=c_send.at[k], recv_sem=c_recv.at[k],
             device_id=source(k), device_id_type=MESH,
         )
@@ -191,17 +200,21 @@
             got = nn(put, part) + nn(put_end, cot[:, DY_TAIL:])
             xs[rows, j * DY_TAIL : (j + 1) * DY_TAIL] = got.astype(BF16)
 
-    dispatch(0)
-    loop(1, 8, lambda k: x_copy(k).start())
-    loop(1, 3, dispatch)
-
-    def two(i):
-        x_copy(8 + i).start()
-        x_copy(16 + (i + 4) % 8).start()
-
-    loop(0, 8, two)
-    dispatch(3)
-    loop(24, 32, lambda k: x_copy(k).start())
+    def ring(chunk, act):
+        def some(i):
+            for q in (1, 2, 3, 0):
+                k = chunk * 16 + q * 4 + (i + q) % 4
+                if q == 0:
+                    pl.when(k > 0)(functools.partial(act, k))
+                else:
+                    act(k)
+
+        loop(0, 4, some)
+
+    loop(0, 2, dispatch)
+    ring(0, lambda k: x_copy(k).start())
+    loop(2, 4, dispatch)
+    ring(1, lambda k: x_copy(k).start())
     xr[0:BLOCK, :] = xs[0:BLOCK, :]
 
     up, down, across = [], [], []
@@ -293,14 +306,11 @@
             both = jnp.where(keep, grad(j * G_TAIL), moved).astype(BF16)
             gs[rows, j * G_TAIL : (j + 1) * G_TAIL] = both
 
-        def give(i):
-            for k in (chunk * 16 + i, chunk * 16 + 8 + (i + 4) % 8):
-                @pl.when(k > 0)
-                def _():
-                    g_copy(k).start()
-                    c_copy(k).start()
-
-        loop(0, 8, give)
+        def give(k):
+            g_copy(k).start()
+            c_copy(k).start()
+
+        ring(chunk, give)
 
     loop(0, 2, work)
     gr[0:BLOCK, :] = gs[0:BLOCK, :]
@@ -308,66 +318,64 @@
 
     loads[3].wait()
     c0, c1 = column(cmb[0:1, :])[:, 0:1], column(cmb[1:2, :])[:, 0:1]
-    col = lane % BLOCK
-
-    def gather(group, carry):
-        def arrived(k):
-            g_copy(k).wait_recv()
-            c_copy(k).wait_recv()
-
-        loop(jnp.where(group == 0, 1, group * 8), group * 8 + 8, arrived)
-        rows = pl.ds(pl.multiple_of(group * ROWS, ROWS), ROWS)
+    first, second = first[:, 0:1], second[:, 0:1]
+    wide_lane = iota((ROWS, WIDE), 1)
+    col = wide_lane % BLOCK
+
+    def arrived(k):
+        g_copy(k).wait_recv()
+        c_copy(k).wait_recv()
+
+    def gone(k):
+        g_copy(k).wait_send()
+        c_copy(k).wait_send()
+
+    def gather(chunk, sums):
+        rows = slice(chunk * WIDE, (chunk + 1) * WIDE)
         v = vx[:, rows].astype(jnp.int32)
-        block = group * 8 + lane // BLOCK
+        block = chunk * 16 + wide_lane // BLOCK
         at0, at1 = first == block, second == block
+        scale = jnp.where(at0, c0, c1)
         hit = (v == col) & (col < CAP)
-        hit0, hit1 = hit & at0, hit & at1
+        put = jnp.where(hit, scale, 0.0).astype(BF16)
+        hit0 = jnp.where(hit & at0, 1.0, 0.0)
+        hit1 = jnp.where(hit & at1, 1.0, 0.0)
+        loop(max(1, chunk * 16), chunk * 16 + 16, arrived)
         end = jnp.zeros((ROWS, G_TAIL), F32)
         for j in range(3):
             cols = slice(j * G_TAIL, (j + 1) * G_TAIL)
-            part = gr[rows, cols]
-            got = c0 * nn(one(hit0), part) + c1 * nn(one(hit1), part)
             hit_end = (v == 3 * (col - CAP) + j) & (col >= CAP)
-            end = end + c0 * nn(one(hit_end & at0), part) + c1 * nn(one(hit_end & at1), part)
-
-            @pl.when(group == 0)
-            def _():
-                home[:, cols] = got
-
-            @pl.when(group > 0)
-            def _():
-                home[:, cols] += got
-
-        @pl.when(group == 0)
-        def _():
+            put_end = jnp.where(hit_end, scale, 0.0).astype(BF16)
+            got = nn(jnp.concatenate([put, put_end], axis=0), gr[rows, cols])
+            end = end + got[ROWS:, :]
+            if chunk == 0:
+                home[:, cols] = got[:ROWS, :]
+            else:
+                out[:, cols] = (home[:, cols] + got[:ROWS, :]).astype(BF16)
+        if chunk == 0:
             home[:, BACK:D] = end
-
-        @pl.when(group > 0)
-        def _():
-            home[:, BACK:D] += end
-
-        line = jnp.zeros((1, ROWS), F32)
-        for i in range(8):
-            line = jnp.where(iota((1, ROWS), 1) // BLOCK == i, cr[group * 8 + i], line)
-        g0, g1 = carry
-        g0 = g0 + jnp.sum(jnp.where(hit0, line, 0.0), axis=1, keepdims=True)
-        g1 = g1 + jnp.sum(jnp.where(hit1, line, 0.0), axis=1, keepdims=True)
+        else:
+            out[:, BACK:D] = (home[:, BACK:D] + end).astype(BF16)
+        g0, g1 = sums
+        for h in range(2):
+            line = jnp.zeros((1, ROWS), F32)
+            for i in range(8):
+                mine = iota((1, ROWS), 1) // BLOCK == i
+                line = jnp.where(mine, cr[chunk * 16 + h * 8 + i], line)
+            part = slice(h * ROWS, (h + 1) * ROWS)
+            g0 = g0 + jnp.sum(hit0[:, part] * line, axis=1, keepdims=True)
+            g1 = g1 + jnp.sum(hit1[:, part] * line, axis=1, keepdims=True)
         return g0, g1
 
+    loop(1, BLOCKS, lambda k: x_copy(k).wait_send())
+    for copy in started:
+        copy.wait_send()
     zero = jnp.zeros((ROWS, 1), F32)
-    g0, g1 = lax.fori_loop(0, GROUPS, gather, (zero, zero))
-    out[...] = home[...].astype(BF16)
+    sums = gather(0, (zero, zero))
+    loop(1, BLOCKS, gone)
+    g0, g1 = gather(1, sums)
     gcomb[0:1, :] = jnp.transpose(jnp.broadcast_to(g0, (ROWS, ROWS)))[0:1, :]
     gcomb[1:2, :] = jnp.transpose(jnp.broadcast_to(g1, (ROWS, ROWS)))[0:1, :]
-
-    def finish(k):
-        x_copy(k).wait_send()
-        g_copy(k).wait_send()
-        c_copy(k).wait_send()
-
-    loop(1, BLOCKS, finish)
-    for copy in started:
-        copy.wait_send()
 
 
 def body(tokens, cotangent, expert_weights, route_ids, combine):

time: 129 us -> 128 us (level)
  no operation moved by 1% of the time
where the time goes in v3:
time: 128 us; the launch traced here: 127 us
  Pallas kernels  124 us (97%)
  local copies, waits for them, and re-layouts  2.45 us (2%)
    pallas_call x1, Pallas kernels, body(): pl.pallas_call(kernel, out_shape=(jax.ShapeDtypeStruct((ROWS, D), BF16),...  124 us

profile of v3, /device:TPU:5, one launch (start us, length us, event | category | flops | bytes accessed | tf_op | source)
XLA Modules:
  0.0 127.4 jit_solution(15810034381070492232)
XLA Ops:
  0.6 124.3 %shard_map.68 = (bf16[128,2048]{1,0:T(8,128)(2,1)}, f32[2,128]{1,0:T(2,128)}) custom-call(bf16[128,2048]{1,0:T(8,128)(2,1)} %tok_hbm.1, bf16[128,2048]{1,0:T(8,128)(2,1)} %cot_hbm.1, bf16[48,6144]{1,0:T(8,128)(2,1)} %bitcast.5, s32[2,128]{1,0:T(2,128)} %bitcast.6, f32[2,128]{1,0:T(2,128)} %bitcast.7), custom_call_target="tpu_custom_call" | custom-call | flops 8589934592 | bytes 4194304 | tf_op jit(solution)/shard_map/pallas_call | solution.py:386
  124.9 0.0 copy-start
  125.0 1.9 %copy.9 = bf16[128,2048]{1,0:T(8,128)(2,1)} copy(bf16[128,2048]{1,0:T(8,128)(2,1)} %get-tuple-element.8) | data formatting | bytes 1048576
  126.8 0.0 copy-done
  126.8 0.6 copy.10
Async XLA Ops:
  124.9 1.9 %copy-start = (f32[2,128]{1,0:T(2,128)S(1)}, f32[2,128]{1,0:T(2,128)}, u32[]{:S(2)}) copy-start(f32[2,128]{1,0:T(2,128)} %get-tuple-element.5) | copy-start | bytes 3076

commit v4 on v3

--- a/solution.py
+++ b/solution.py
@@ -54,7 +54,7 @@
 
 
 def steps(k):
-    return table(k // 4, (0, 4, 3, 5, 1, 7, 2, 6)), k % 4
+    return table(k // 4, (0, 4, 3, 5, 2, 6, 1, 7)), k % 4
 
 
 def iota(shape, dim):
@@ -114,7 +114,7 @@
     ids = rid[...]
     step_z = (ids // NY - z % 4 + 4) % 4
     step_y = (ids % NY - y + NY) % NY
-    rel = (table(step_y, (0, 4, 6, 2, 1, 3, 7, 5)) * 4 + step_z).astype(F32)
+    rel = (table(step_y, (0, 6, 4, 2, 1, 3, 5, 7)) * 4 + step_z).astype(F32)
 
     def column(line):
         return jnp.transpose(jnp.broadcast_to(line, (ROWS, ROWS)))
@@ -202,7 +202,7 @@
 
     def ring(chunk, act):
         def some(i):
-            for q in (1, 2, 3, 0):
+            for q in (2, 3, 1, 0):
                 k = chunk * 16 + q * 4 + (i + q) % 4
                 if q == 0:
                     pl.when(k > 0)(functools.partial(act, k))

time: 128 us -> 127 us (level)
    pallas_call x1, Pallas kernels: 124 us -> 123 us  [body(): pl.pallas_call(kernel, out_shape=(jax.ShapeDtypeStruct((ROWS, D), BF16),...]
where the time goes in v4:
time: 127 us; the launch traced here: 126 us
  Pallas kernels  123 us (97%)
  local copies, waits for them, and re-layouts  2.45 us (2%)
    pallas_call x1, Pallas kernels, body(): pl.pallas_call(kernel, out_shape=(jax.ShapeDtypeStruct((ROWS, D), BF16),...  123 us

profile of v4, /device:TPU:5, one launch (start us, length us, event | category | flops | bytes accessed | tf_op | source)
XLA Modules:
  0.0 126.1 jit_solution(2364775878130905864)
XLA Ops:
  0.6 123.0 %shard_map.68 = (bf16[128,2048]{1,0:T(8,128)(2,1)}, f32[2,128]{1,0:T(2,128)}) custom-call(bf16[128,2048]{1,0:T(8,128)(2,1)} %tok_hbm.1, bf16[128,2048]{1,0:T(8,128)(2,1)} %cot_hbm.1, bf16[48,6144]{1,0:T(8,128)(2,1)} %bitcast.5, s32[2,128]{1,0:T(2,128)} %bitcast.6, f32[2,128]{1,0:T(2,128)} %bitcast.7), custom_call_target="tpu_custom_call" | custom-call | flops 8589934592 | bytes 4194304 | tf_op jit(solution)/shard_map/pallas_call | solution.py:386
  123.6 0.0 copy-start
  123.6 1.9 %copy.9 = bf16[128,2048]{1,0:T(8,128)(2,1)} copy(bf16[128,2048]{1,0:T(8,128)(2,1)} %get-tuple-element.8) | data formatting | bytes 1048576
  125.5 0.0 copy-done
  125.5 0.6 copy.10
Async XLA Ops:
  123.6 1.9 %copy-start = (f32[2,128]{1,0:T(2,128)S(1)}, f32[2,128]{1,0:T(2,128)}, u32[]{:S(2)}) copy-start(f32[2,128]{1,0:T(2,128)} %get-tuple-element.5) | copy-start | bytes 3076
